TPU v7x, 32 devices: a whole 2x2x4 slice. The times are simulated.
32 devices in a mesh: dom: 16 (over z, y, x), feat: 2 (over core).
Axes of the slice: x: 2, y: 2, z: 4, core: 2. Of those that a mesh axis runs over, the one named last changes fastest.
Arguments:
- features: bfloat16 [32768, 100], P('dom', 'feat'), may hold values from -6 to 6
- local_mask: int32 [32768, 2048], P('dom'), may hold values 0 or 1
- halo_mask: int32 [32768, 128], P('dom'), may hold values 0 or 1
- send_rows: int32 [16, 16, 8], P('dom'), may hold values from 0 to 2047
- labels: int32 [32768], P('dom'), may hold values from 0 to 46
- label_mask: int32 [32768], P('dom'), may hold values from 0 to 1
- master: float32 [2, 103680], P('feat', 'dom')
- first_moment: float32 [2, 103680], P('feat', 'dom'), may hold values from -0.00390625 to 0.00390625
- second_moment: float32 [2, 103680], P('feat', 'dom'), may hold values from 6.866455e-09 to 2.746582e-08
Outputs:
- loss_sum: float32 [], replicated
- label_count: float32 [], replicated
- new_master: float32 [2, 103680], P('feat', 'dom')
- new_first: float32 [2, 103680], P('feat', 'dom')
- new_second: float32 [2, 103680], P('feat', 'dom')
All inputs are finite; a program needn't handle non-finite values. No bound on the sum of `local_mask` or of `halo_mask` on one device may be relied on, other than what follows from the above.
Results may differ from a plain program's by a relative error of at most 0.0005.
The roundings to bfloat16 on the way count: a program that leaves them out, or rounds other values in their place, can miss the bound.
Values may be sent and summed in bfloat16 or wider, within the bound.
A program may use at most 128 MiB of HBM per device.

v0:
```python
import jax
import jax.numpy as jnp
from jax import lax
from jax.sharding import PartitionSpec as P

HID = 256
CLS = 47
STEP = 10
EPSILON = 1e-05
LEARN_RATE = 0.02
DECAY_ONE = 0.9
DECAY_TWO = 0.999
ADAM_EPS = 1e-08
WEIGHT_DECAY = 0.01


def product(matrix_a, matrix_b):
    return jnp.dot(matrix_a, matrix_b, preferred_element_type=jnp.float32)


def contract_rows(matrix_a, matrix_b):
    return lax.dot_general(
        matrix_a, matrix_b, (((0,), (0,)), ((), ())), preferred_element_type=jnp.float32
    )


def contract_cols(matrix_a, matrix_b):
    return lax.dot_general(
        matrix_a, matrix_b, (((1,), (1,)), ((), ())), preferred_element_type=jnp.float32
    )


def unpack(flat_params, inner_width, hidden_width):
    edge_one = 2 * inner_width * HID
    edge_two = edge_one + 2 * hidden_width * HID
    edge_three = edge_two + 2 * hidden_width * CLS
    layer_one = flat_params[:edge_one].reshape(2, inner_width, HID)
    layer_two = flat_params[edge_one:edge_two].reshape(2, hidden_width, HID)
    head_part = flat_params[edge_two:edge_three].reshape(2, hidden_width, CLS)
    norm_part = flat_params[edge_three:].reshape(4, hidden_width)
    matrices = [
        (layer_one[0], layer_one[1]),
        (layer_two[0], layer_two[1]),
        (head_part[0], head_part[1]),
    ]
    return (matrices, norm_part)


def layer_forward(states, weight_pair, graph, is_head):
    local_adj, halo_adj, inverse, send_index = graph
    outgoing = jnp.take(states, send_index, axis=0)
    incoming = lax.all_to_all(outgoing, "dom", split_axis=0, concat_axis=0, tiled=True)
    halo_feats = incoming.reshape(-1, states.shape[1])
    summed = product(local_adj, states) + product(halo_adj, halo_feats)
    aggregated = (summed * inverse[:, None]).astype(jnp.bfloat16)
    if is_head:
        partial_value = product(states, weight_pair[0]) + product(aggregated, weight_pair[1])
        mixed = lax.psum(partial_value, "feat")
    else:
        partial_value = product(states, weight_pair[0]) + product(aggregated, weight_pair[1])
        mixed = lax.psum_scatter(partial_value, "feat", scatter_dimension=1, tiled=True)
    return (mixed, aggregated)


def norm_forward(mixed, gain, shift):
    totals = lax.psum((jnp.sum(mixed, axis=1), jnp.sum(mixed * mixed, axis=1)), "feat")
    centre_mean = totals[0] / HID
    variance = totals[1] / HID - centre_mean * centre_mean
    scale_inv = lax.rsqrt(variance + EPSILON)
    normed = (mixed - centre_mean[:, None]) * scale_inv[:, None]
    shifted = normed * gain + shift
    return (jax.nn.gelu(shifted).astype(jnp.bfloat16), (normed, scale_inv, shifted))


def norm_backward(grad_out, kept, gain):
    normed, scale_inv, shifted = kept
    unused, gelu_back = jax.vjp(jax.nn.gelu, shifted)
    grad_shift = gelu_back(grad_out)[0]
    grad_gain = jnp.sum(grad_shift * normed, axis=0)
    grad_bias = jnp.sum(grad_shift, axis=0)
    grad_normed = grad_shift * gain
    totals = lax.psum((jnp.sum(grad_normed, axis=1), jnp.sum(grad_normed * normed, axis=1)), "feat")
    grad_mixed = scale_inv[:, None] * (
        grad_normed - totals[0][:, None] / HID - normed * totals[1][:, None] / HID
    )
    return (grad_mixed, grad_gain, grad_bias)


def layer_backward(grad_full, states, aggregated, weight_pair, graph, needs_input):
    grad_self = contract_rows(states, grad_full)
    grad_neigh = contract_rows(aggregated, grad_full)
    if not needs_input:
        return (grad_self, grad_neigh, None)
    local_adj, halo_adj, inverse, send_index = graph
    grad_states = contract_cols(grad_full, weight_pair[0])
    grad_agg = contract_cols(grad_full, weight_pair[1])
    grad_summed = (grad_agg * inverse[:, None]).astype(jnp.bfloat16)
    grad_states = grad_states + contract_rows(local_adj, grad_summed)
    grad_halo = contract_rows(halo_adj, grad_summed).astype(jnp.bfloat16)
    returned = lax.all_to_all(
        grad_halo.reshape(send_index.shape + (-1,)), "dom", split_axis=0, concat_axis=0, tiled=True
    )
    flat_back = returned.reshape(-1, returned.shape[-1]).astype(jnp.float32)
    grad_states = grad_states.at[send_index.reshape(-1)].add(flat_back)
    return (grad_self, grad_neigh, grad_states)


def per_device(
    features,
    local_mask,
    halo_mask,
    send_rows,
    labels,
    label_mask,
    master,
    first_moment,
    second_moment,
):
    gathered = lax.all_gather(master.astype(jnp.bfloat16), "dom", axis=1, tiled=True)
    inner_width = features.shape[1]
    hidden_width = HID // lax.axis_size("feat")
    matrices, norm_part = unpack(gathered[0], inner_width, hidden_width)
    norm_float = norm_part.astype(jnp.float32)
    local_adj = local_mask.astype(jnp.bfloat16)
    halo_adj = halo_mask.astype(jnp.bfloat16)
    degree = jnp.sum(local_mask, axis=1) + jnp.sum(halo_mask, axis=1)
    inverse = 1.0 / jnp.maximum(degree, 1).astype(jnp.float32)
    graph = (local_adj, halo_adj, inverse, send_rows[0])
    weight_mask = label_mask.astype(jnp.float32)
    states = features
    inputs_kept = []
    norms_kept = []
    for number in range(3):
        mixed, aggregated = layer_forward(states, matrices[number], graph, number == 2)
        inputs_kept.append((states, aggregated))
        if number < 2:
            states, kept = norm_forward(mixed, norm_float[2 * number], norm_float[2 * number + 1])
            norms_kept.append(kept)
    log_total = jax.nn.logsumexp(mixed, axis=1)
    classes = lax.broadcasted_iota(jnp.int32, mixed.shape, 1)
    onehot = (classes == labels[:, None]).astype(jnp.float32)
    picked = jnp.sum(mixed * onehot, axis=1)
    loss_sum, label_count = lax.psum(
        (jnp.sum((log_total - picked) * weight_mask), jnp.sum(weight_mask)), "dom"
    )
    probs = jnp.exp(mixed - log_total[:, None])
    grad_full = ((probs - onehot) * (weight_mask / label_count)[:, None]).astype(jnp.bfloat16)
    weight_grads = [None, None, None]
    norm_grads = [None, None]
    for number in (2, 1, 0):
        states, aggregated = inputs_kept[number]
        grad_self, grad_neigh, grad_states = layer_backward(
            grad_full, states, aggregated, matrices[number], graph, number > 0
        )
        weight_grads[number] = (grad_self, grad_neigh)
        if number > 0:
            grad_mixed, grad_gain, grad_bias = norm_backward(
                grad_states, norms_kept[number - 1], norm_float[2 * number - 2]
            )
            norm_grads[number - 1] = (grad_gain, grad_bias)
            grad_full = lax.all_gather(grad_mixed.astype(jnp.bfloat16), "feat", axis=1, tiled=True)
    pieces = [
        weight_grads[0][0],
        weight_grads[0][1],
        weight_grads[1][0],
        weight_grads[1][1],
        weight_grads[2][0],
        weight_grads[2][1],
        norm_grads[0][0],
        norm_grads[0][1],
        norm_grads[1][0],
        norm_grads[1][1],
    ]
    gradient = jnp.concatenate([piece.reshape(-1) for piece in pieces])[None, :]
    shard_width = master.shape[1]
    summed_all = lax.psum(gradient, "dom")
    own_grad = lax.dynamic_slice_in_dim(
        summed_all, lax.axis_index("dom") * shard_width, shard_width, 1
    )
    new_first = DECAY_ONE * first_moment + (1.0 - DECAY_ONE) * own_grad
    new_second = DECAY_TWO * second_moment + (1.0 - DECAY_TWO) * own_grad * own_grad
    first_hat = new_first / (1.0 - DECAY_ONE**STEP)
    second_hat = new_second / (1.0 - DECAY_TWO**STEP)
    new_master = master - LEARN_RATE * (
        first_hat / (jnp.sqrt(second_hat) + ADAM_EPS) + WEIGHT_DECAY * master
    )
    return (loss_sum, label_count, new_master, new_first, new_second)


def solution(mesh):
    in_specs = (
        P("dom", "feat"),
        P("dom", None),
        P("dom", None),
        P("dom", None, None),
        P("dom"),
        P("dom"),
        P("feat", "dom"),
        P("feat", "dom"),
        P("feat", "dom"),
    )
    out_specs = (P(), P(), P("feat", "dom"), P("feat", "dom"), P("feat", "dom"))
    return jax.shard_map(
        per_device, mesh=mesh, in_specs=in_specs, out_specs=out_specs, check_vma=False
    )
```

profile of v0, /device:TPU:0, one launch (start us, length us, event | category | flops | bytes accessed | tf_op | source)
XLA Modules:
  0.0 488.4 jit_solution(10697952890645526541)
XLA Ops:
  11.6 8.3 %all-to-all-start = ((bf16[16,2,200]{2,1,0:T(2,128)(2,1)}), bf16[16,2,200]{2,1,0:T(2,128)(2,1)S(1)}, u32[]{:S(2)}, u32[]{:S(2)}) async-start(bf16[16,2,200]{2,1,0:T(2,128)(2,1)} %reshape.262), calls=%async_computation | async-start | bytes 32768 | tf_op jit(solution)/shard_map/all_to_all | solution.py:52
  23.9 13.5 %fusion.39 = (s32[2048]{0:T(1024)S(1)}, bf16[2048,2048]{1,0:T(8,128)(2,1)S(1)}) fusion(s32[2048,2048]{1,0:T(8,128)} %param.12), kind=kLoop, calls=%fused_computation.129 | loop fusion | flops 8386560 | bytes 25174016 | tf_op jit(solution)/shard_map/reduce_sum | solution.py:126
  37.8 2.9 copy-done
  40.7 2.7 fusion.41
  43.9 89.5 %all-reduce.14.cloned.1.call-done = bf16[103680]{0:T(1024)(128)(2,1)} async-done(((bf16[103680]{0:T(1024)(128)(2,1)}), bf16[103680]{0:T(1024)(128)(2,1)}) %all-reduce.14.cloned.1.call-update) | async-done | bytes 207376
  136.7 1.9 convolution_add_fusion
  141.3 6.8 %reduce-scatter.3.cloned.1.call-done = f32[2048,128]{0,1:T(8,128)} async-done(((f32[2048,256]{0,1:T(8,128)}), f32[2048,128]{0,1:T(8,128)}) %reduce-scatter.3.cloned.1.call-update) | async-done | bytes 1048592 | tf_op jit(solution)/shard_map/reduce_scatter | solution.py:61
  148.1 1.4 fusion.35
  149.4 3.3 all-reduce.5
  152.8 1.8 multiply_convert_fusion.3
  154.6 7.5 %fusion.43 = f32[128,2048]{1,0:T(8,128)} fusion(bf16[2048,128]{0,1:T(8,128)(2,1)S(1)} %multiply_convert_fusion.3, bf16[2048,2048]{1,0:T(8,128)(2,1)} %copy-done), kind=kOutput, calls=%fused_computation.133 | convolution fusion | flops 1073741824 | bytes 9961472 | tf_op jit(solution)/shard_map/dot_general | solution.py:18
  163.8 6.9 %all-to-all-start.1 = ((bf16[16,8,128]{2,1,0:T(8,128)(2,1)}), bf16[16,8,128]{2,1,0:T(8,128)(2,1)S(1)}, u32[]{:S(2)}, u32[]{:S(2)}) async-start(bf16[16,8,128]{2,1,0:T(8,128)(2,1)} %bitcast_select_fusion.1), calls=%async_computation.2 | async-start | bytes 65536 | tf_op jit(solution)/shard_map/all_to_all | solution.py:52
  172.3 5.8 %all-to-all-done.1 = bf16[16,8,128]{2,1,0:T(8,128)(2,1)S(1)} async-done(((bf16[16,8,128]{2,1,0:T(8,128)(2,1)}), bf16[16,8,128]{2,1,0:T(8,128)(2,1)S(1)}, u32[]{:S(2)}, u32[]{:S(2)}) %all-to-all-start.1) | async-done | bytes 32800 | tf_op jit(solution)/shard_map/all_to_all | solution.py:52
  178.1 1.5 fusion.3
  180.5 2.7 convolution_add_fusion.1
  184.6 5.0 %reduce-scatter.5.cloned.1.call-done = f32[2048,128]{0,1:T(8,128)} async-done(((f32[2048,256]{0,1:T(8,128)}), f32[2048,128]{0,1:T(8,128)}) %reduce-scatter.5.cloned.1.call-update) | async-done | bytes 1048592 | tf_op jit(solution)/shard_map/reduce_scatter | solution.py:61
  190.9 3.3 all-reduce.4
  194.3 1.8 multiply_convert_fusion.2
  196.1 6.3 %fusion.45 = f32[128,2048]{1,0:T(8,128)S(1)} fusion(bf16[2048,128]{0,1:T(8,128)(2,1)S(1)} %multiply_convert_fusion.2, bf16[2048,2048]{1,0:T(8,128)(2,1)} %copy-done), kind=kOutput, calls=%fused_computation.135 | convolution fusion | flops 1073741824 | bytes 9961472 | tf_op jit(solution)/shard_map/dot_general | solution.py:18
  204.1 6.9 %all-to-all-start.2 = ((bf16[16,8,128]{2,1,0:T(8,128)(2,1)}), bf16[16,8,128]{2,1,0:T(8,128)(2,1)S(1)}, u32[]{:S(2)}, u32[]{:S(2)}) async-start(bf16[16,8,128]{2,1,0:T(8,128)(2,1)} %bitcast_select_fusion), calls=%async_computation.4 | async-start | bytes 65536 | tf_op jit(solution)/shard_map/all_to_all | solution.py:52
  211.2 7.1 %all-to-all-done.2 = bf16[16,8,128]{2,1,0:T(8,128)(2,1)S(1)} async-done(((bf16[16,8,128]{2,1,0:T(8,128)(2,1)}), bf16[16,8,128]{2,1,0:T(8,128)(2,1)S(1)}, u32[]{:S(2)}, u32[]{:S(2)}) %all-to-all-start.2) | async-done | bytes 32800 | tf_op jit(solution)/shard_map/all_to_all | solution.py:52
  220.7 15.0 %all-reduce.10.cloned.1.call-done = f32[2048,47]{0,1:T(8,128)} async-done(((f32[2048,47]{0,1:T(8,128)}), f32[2048,47]{0,1:T(8,128)}) %all-reduce.10.cloned.1.call-update) | async-done | bytes 385040 | tf_op jit(solution)/shard_map/psum | solution.py:58
  238.5 42.6 %all-reduce.1 = (f32[]{:T(128)}, f32[]{:T(128)}) all-reduce(f32[]{:T(128)} %get-tuple-element.27, f32[]{:T(128)} %get-tuple-element.26), channel_id=1, replica_groups=mesh['dom'=16,'feat'=2] {'dom'}, use_global_device_ids=true, to_apply=%region_17.19 | all-reduce | flops 2 | bytes 16 | tf_op jit(solution)/shard_map/psum | solution.py:143
  283.4 7.9 %convolution_bitcast_fusion.2 = f32[2048,128]{1,0:T(8,128)} fusion(bf16[2048,128]{1,0:T(8,128)(2,1)S(1)} %fusion.5, bf16[2048,2048]{1,0:T(8,128)(2,1)} %copy-done), kind=kOutput, calls=%fused_computation.9 | convolution fusion | flops 1073741824 | bytes 9961472 | tf_op jit(solution)/shard_map/dot_general | solution.py:22
  292.2 3.5 all-to-all-start.3
  295.8 1.6 convolution_add_fusion.2
  297.3 5.8 %all-to-all-done.3 = bf16[16,8,128]{2,1,0:T(8,128)(2,1)S(1)} async-done(((bf16[16,8,128]{2,1,0:T(8,128)(2,1)}), bf16[16,8,128]{2,1,0:T(8,128)(2,1)S(1)}, u32[]{:S(2)}, u32[]{:S(2)}) %all-to-all-start.3) | async-done | bytes 32800 | tf_op jit(solution)/shard_map/all_to_all | solution.py:100
  303.1 1.9 scatter_custom_fusion
  305.0 1.4 copy.45
  306.4 3.0 multiply_reduce_fusion
  309.3 3.4 all-reduce.3
  313.9 5.7 %all-gather.3.cloned.1.call-done = bf16[2048,256]{0,1:T(8,128)(2,1)} async-done(((bf16[2048,128]{0,1:T(8,128)(2,1)}), bf16[2048,256]{0,1:T(8,128)(2,1)}) %all-gather.3.cloned.1.call-update) | async-done | bytes 1048592 | tf_op jit(solution)/shard_map/all_gather | solution.py:161
  319.6 2.0 fusion.2
  321.6 7.8 %convolution_bitcast_fusion.1 = f32[2048,128]{1,0:T(8,128)} fusion(bf16[2048,128]{1,0:T(8,128)(2,1)S(1)} %fusion.2, bf16[2048,2048]{1,0:T(8,128)(2,1)} %copy-done), kind=kOutput, calls=%fused_computation.8 | convolution fusion | flops 1073741824 | bytes 9961472 | tf_op jit(solution)/shard_map/dot_general | solution.py:22
  330.3 6.9 %all-to-all-start.4 = ((bf16[16,8,128]{2,1,0:T(8,128)(2,1)}), bf16[16,8,128]{2,1,0:T(8,128)(2,1)S(1)}, u32[]{:S(2)}, u32[]{:S(2)}) async-start(bf16[16,8,128]{2,1,0:T(8,128)(2,1)} %fusion.10), calls=%async_computation.6 | async-start | bytes 65536 | tf_op jit(solution)/shard_map/all_to_all | solution.py:100
  337.3 2.7 convolution_add_fusion.5
  340.0 4.6 all-to-all-done.4
  344.7 3.5 scatter_custom_fusion.1
  348.1 2.6 copy.48
  350.8 3.3 multiply_reduce_fusion.1
  354.1 3.3 all-reduce.2
  357.4 2.3 multiply_convert_fusion
  362.1 1.6 convolution_bitcast_fusion.4
  364.3 1.4 all-gather.5.cloned.1.call-done
  365.7 1.8 fusion.46
  367.5 1.7 convolution_bitcast_fusion.6
  370.5 109.5 %all-reduce.12.cloned.1.call-done = f32[1,103680]{1,0:T(1,128)} async-done(((f32[1,103680]{1,0:T(1,128)}), f32[1,103680]{1,0:T(1,128)}) %all-reduce.12.cloned.1.call-update) | async-done | bytes 414736 | tf_op jit(solution)/shard_map/psum | solution.py:176
  480.0 1.6 multiply_subtract_fusion
  (154 shorter events, 37.9 us)
Async XLA Ops:
  11.6 31.8 %all-to-all-start = ((bf16[16,2,200]{2,1,0:T(2,128)(2,1)}), bf16[16,2,200]{2,1,0:T(2,128)(2,1)S(1)}, u32[]{:S(2)}, u32[]{:S(2)}) async-start(bf16[16,2,200]{2,1,0:T(2,128)(2,1)} %reshape.262), calls=%async_computation | async-start | bytes 32768 | tf_op jit(solution)/shard_map/all_to_all | solution.py:52
  19.9 113.5 %all-reduce.14.cloned.1.call-start = ((), (), s32[]{:S(2)}) async-start(), calls=%async_computation.13 | async-start | bytes 417792
  23.1 0.7 copy-start.12
  23.8 13.6 %copy-start.11 = (s32[2048,128]{1,0:T(8,128)S(1)}, s32[2048,128]{1,0:T(8,128)}, u32[]{:S(2)}) copy-start(s32[2048,128]{1,0:T(8,128)} %param.13) | copy-start | bytes 3145732
  23.8 16.8 %copy-start.8 = (bf16[2048,50]{0,1:T(8,128)(2,1)S(1)}, bf16[2048,50]{0,1:T(8,128)(2,1)}, u32[]{:S(2)}) copy-start(bf16[2048,50]{0,1:T(8,128)(2,1)} %param.11) | copy-start | bytes 614404
  23.8 124.3 %reduce-scatter.3.cloned.1.call-start = ((), (), s32[]{:S(2)}) async-start(), calls=%async_computation.7 | async-start | bytes 3145728 | tf_op jit(solution)/shard_map/reduce_scatter | solution.py:61
  37.4 3.2 copy-start
  43.3 95.3 %copy-start.16 = (s32[1,16,8]{1,2,0:T(8,128)S(1)}, s32[1,16,8]{1,2,0:T(8,128)}, u32[]{:S(2)}) copy-start(s32[1,16,8]{1,2,0:T(8,128)} %param.14) | copy-start | bytes 1540
  43.9 118.3 %copy-start.9 = (bf16[2048,50]{0,1:T(8,128)(2,1)}, bf16[2048,50]{0,1:T(8,128)(2,1)S(1)}, u32[]{:S(2)}) copy-start(bf16[2048,50]{0,1:T(8,128)(2,1)S(1)} %fusion.8) | copy-start | bytes 614404
  134.6 27.6 %copy-start.10 = (bf16[1,103680]{1,0:T(2,128)(2,1)}, bf16[1,103680]{1,0:T(2,128)(2,1)S(1)}, u32[]{:S(2)}) copy-start(bf16[1,103680]{1,0:T(2,128)(2,1)S(1)} %reshape.240) | copy-start | bytes 622084
  141.3 30.9 %copy-start.21 = (f32[128]{0:T(128)}, f32[128]{0:T(128)S(1)}, u32[]{:S(2)}) copy-start(f32[128]{0:T(128)S(1)} %get-tuple-element.54) | copy-start | bytes 1540
  154.6 28.6 %copy-start.4 = (bf16[2048,128]{0,1:T(8,128)(2,1)}, bf16[2048,128]{0,1:T(8,128)(2,1)S(1)}, u32[]{:S(2)}) copy-start(bf16[2048,128]{0,1:T(8,128)(2,1)S(1)} %multiply_convert_fusion.3) | copy-start | bytes 1572868
  162.4 31.8 %copy-start.23 = (f32[128]{0:T(128)S(1)}, f32[128]{0:T(128)}, u32[]{:S(2)}) copy-start(f32[128]{0:T(128)} %get-tuple-element.53) | copy-start | bytes 1540
  163.8 14.3 %all-to-all-start.1 = ((bf16[16,8,128]{2,1,0:T(8,128)(2,1)}), bf16[16,8,128]{2,1,0:T(8,128)(2,1)S(1)}, u32[]{:S(2)}, u32[]{:S(2)}) async-start(bf16[16,8,128]{2,1,0:T(8,128)(2,1)} %bitcast_select_fusion.1), calls=%async_computation.2 | async-start | bytes 65536 | tf_op jit(solution)/shard_map/all_to_all | solution.py:52
  170.7 18.8 %reduce-scatter.5.cloned.1.call-start = ((), (), s32[]{:S(2)}) async-start(), calls=%async_computation.8 | async-start | bytes 3145728 | tf_op jit(solution)/shard_map/reduce_scatter | solution.py:61
  179.7 0.8 copy-start.6
  196.1 40.7 %copy-start.17 = (s32[2048]{0:T(1024)S(1)}, s32[2048]{0:T(1024)}, u32[]{:S(2)}) copy-start(s32[2048]{0:T(1024)} %param.15) | copy-start | bytes 24580
  196.1 41.8 %copy-start.18 = (s32[2048]{0:T(1024)S(1)}, s32[2048]{0:T(1024)}, u32[]{:S(2)}) copy-start(s32[2048]{0:T(1024)} %param.16) | copy-start | bytes 24580
  204.1 14.3 %all-to-all-start.2 = ((bf16[16,8,128]{2,1,0:T(8,128)(2,1)}), bf16[16,8,128]{2,1,0:T(8,128)(2,1)S(1)}, u32[]{:S(2)}, u32[]{:S(2)}) async-start(bf16[16,8,128]{2,1,0:T(8,128)(2,1)} %bitcast_select_fusion), calls=%async_computation.4 | async-start | bytes 65536 | tf_op jit(solution)/shard_map/all_to_all | solution.py:52
  210.9 24.8 %all-reduce.10.cloned.1.call-start = ((), (), s32[]{:S(2)}) async-start(), calls=%async_computation.9 | async-start | bytes 786432 | tf_op jit(solution)/shard_map/psum | solution.py:58
  218.7 0.8 copy-start.7
  220.7 84.3 %copy-start.27 = (s32[128]{0:T(128)}, s32[128]{0:T(128)S(1)}, u32[]{:S(2)}) copy-start(s32[128]{0:T(128)S(1)} %fusion.33) | copy-start | bytes 1540
  283.3 23.0 %copy-start.3 = (f32[2048,128]{0,1:T(8,128)S(1)}, f32[2048,128]{0,1:T(8,128)}, u32[]{:S(2)}) copy-start(f32[2048,128]{0,1:T(8,128)} %reduce-scatter.5.cloned.1.call-done) | copy-start | bytes 3145732
  283.3 23.0 %copy-start.24 = (f32[128]{0:T(128)S(1)}, f32[128]{0:T(128)}, u32[]{:S(2)}) copy-start(f32[128]{0:T(128)} %get-tuple-element.53) | copy-start | bytes 1540
  291.3 28.3 %copy-start.13 = (bf16[128,256]{1,0:T(8,128)(2,1)S(1)}, bf16[128,256]{1,0:T(8,128)(2,1)}, u32[]{:S(2)}) copy-start(bf16[128,256]{1,0:T(8,128)(2,1)} %squeeze.29) | copy-start | bytes 196612
  292.2 10.9 %all-to-all-start.3 = ((bf16[16,8,128]{2,1,0:T(8,128)(2,1)}), bf16[16,8,128]{2,1,0:T(8,128)(2,1)S(1)}, u32[]{:S(2)}, u32[]{:S(2)}) async-start(bf16[16,8,128]{2,1,0:T(8,128)(2,1)} %fusion.9), calls=%async_computation.5 | async-start | bytes 65536 | tf_op jit(solution)/shard_map/all_to_all | solution.py:100
  295.7 23.9 %all-gather.3.cloned.1.call-start = ((), (), s32[]{:S(2)}) async-start(), calls=%async_computation.10 | async-start | bytes 1572864 | tf_op jit(solution)/shard_map/all_gather | solution.py:161
  309.3 28.0 %copy-start.14 = (bf16[128,256]{1,0:T(8,128)(2,1)S(1)}, bf16[128,256]{1,0:T(8,128)(2,1)}, u32[]{:S(2)}) copy-start(bf16[128,256]{1,0:T(8,128)(2,1)} %squeeze.28) | copy-start | bytes 196612
  319.6 17.7 %copy-start.1 = (bf16[2048,256]{0,1:T(8,128)(2,1)S(1)}, bf16[2048,256]{0,1:T(8,128)(2,1)}, u32[]{:S(2)}) copy-start(bf16[2048,256]{0,1:T(8,128)(2,1)} %all-gather.3.cloned.1.call-done) | copy-start | bytes 3145732
  321.5 29.2 %copy-start.2 = (f32[2048,128]{0,1:T(8,128)S(1)}, f32[2048,128]{0,1:T(8,128)}, u32[]{:S(2)}) copy-start(f32[2048,128]{0,1:T(8,128)} %reduce-scatter.3.cloned.1.call-done) | copy-start | bytes 3145732
  321.6 29.2 %copy-start.22 = (f32[128]{0:T(128)S(1)}, f32[128]{0:T(128)}, u32[]{:S(2)}) copy-start(f32[128]{0:T(128)} %copy-done.21) | copy-start | bytes 1540
  330.3 33.4 %copy-start.5 = (bf16[2048,128]{0,1:T(8,128)(2,1)S(1)}, bf16[2048,128]{0,1:T(8,128)(2,1)}, u32[]{:S(2)}) copy-start(bf16[2048,128]{0,1:T(8,128)(2,1)} %copy-done.4) | copy-start | bytes 1572868
  330.3 14.3 %all-to-all-start.4 = ((bf16[16,8,128]{2,1,0:T(8,128)(2,1)}), bf16[16,8,128]{2,1,0:T(8,128)(2,1)S(1)}, u32[]{:S(2)}, u32[]{:S(2)}) async-start(bf16[16,8,128]{2,1,0:T(8,128)(2,1)} %fusion.10), calls=%async_computation.6 | async-start | bytes 65536 | tf_op jit(solution)/shard_map/all_to_all | solution.py:100
  337.3 28.4 %all-gather.5.cloned.1.call-start = ((), (), s32[]{:S(2)}) async-start(), calls=%async_computation.11 | async-start | bytes 1572864 | tf_op jit(solution)/shard_map/all_gather | solution.py:161
  350.7 18.6 %copy-start.26 = (f32[128]{0:T(128)S(1)}, f32[128]{0:T(128)}, u32[]{:S(2)}) copy-start(f32[128]{0:T(128)} %get-tuple-element.6) | copy-start | bytes 1540
  350.7 18.6 %copy-start.25 = (f32[128]{0:T(128)S(1)}, f32[128]{0:T(128)}, u32[]{:S(2)}) copy-start(f32[128]{0:T(128)} %get-tuple-element.12) | copy-start | bytes 1540
  350.8 129.2 %copy-start.15 = (f32[1,6480]{1,0:T(1,128)S(1)}, f32[1,6480]{1,0:T(1,128)}, u32[]{:S(2)}) copy-start(f32[1,6480]{1,0:T(1,128)} %param.17) | copy-start | bytes 77764
  350.8 129.2 %copy-start.19 = (f32[1,6480]{1,0:T(1,128)S(1)}, f32[1,6480]{1,0:T(1,128)}, u32[]{:S(2)}) copy-start(f32[1,6480]{1,0:T(1,128)} %param.18) | copy-start | bytes 77764
  350.8 129.2 %copy-start.20 = (f32[1,6480]{1,0:T(1,128)S(1)}, f32[1,6480]{1,0:T(1,128)}, u32[]{:S(2)}) copy-start(f32[1,6480]{1,0:T(1,128)} %param.19) | copy-start | bytes 77764
  359.8 120.2 %all-reduce.12.cloned.1.call-start = ((), (), s32[]{:S(2)}) async-start(), calls=%async_computation.12 | async-start | bytes 829440 | tf_op jit(solution)/shard_map/psum | solution.py:176
Sparse Core Ops, SparseCore 0:
  26.0 107.3 all-reduce.13
  138.7 9.3 reduce-scatter.2
  183.4 6.1 reduce-scatter.4
  220.6 15.0 all-reduce.9
  314.0 5.5 all-gather.2
  359.9 5.7 all-gather.4
  370.9 109.0 all-reduce.11
where the time goes:
time: 490 us; the launch traced here: 488 us
  waiting for transfers between devices  256 us (52%)
  matrix products  57.9 us (12%)
  blocking collectives  55.9 us (11%)
  other arithmetic  45.1 us (9%)
  starting transfers between devices  33.2 us (7%)
  local copies, waits for them, and re-layouts  24.5 us (5%)
  between operations  15.5 us (3%)
    psum x1, waiting for transfers between devices, per_device(): summed_all = lax.psum(gradient, 'dom')  109 us
    unnamed x8, waiting for transfers between devices  89.6 us
    psum x1, blocking collectives, per_device(): lax.psum((jnp.sum((log_total - picked) * weight_mask), jnp.sum(weight_mas...  42.6 us
    dot_general x12, matrix products, product(): return jnp.dot(matrix_a, matrix_b, preferred_element_type=jnp.float32)  26.4 us
    dot_general x10, matrix products, contract_rows(): lax.dot_general(matrix_a, matrix_b, (((0,), (0,)), ((), ())), preferred_e...  24.8 us
    all_to_all x3, starting transfers between devices, layer_forward(): lax.all_to_all(outgoing, 'dom', split_axis=0, concat_axis=0, tiled=True)  22 us
    psum x1, waiting for transfers between devices, layer_forward(): mixed = lax.psum(partial_value, 'feat')  15 us
    reduce_sum x2, other arithmetic, per_device(): degree = jnp.sum(local_mask, axis=1) + jnp.sum(halo_mask, axis=1)  13.9 us
  transfers between devices with their start and end apart: 12, of which 11 were waited for; matrix products, arithmetic and copies ran while one was open for 7% of the time, Pallas kernels for 0%

commit v1 on v0

--- a/solution.py
+++ b/solution.py
@@ -12,6 +12,28 @@
 DECAY_TWO = 0.999
 ADAM_EPS = 1e-08
 WEIGHT_DECAY = 0.01
+
+
+def cut_along(value, dim, size):
+    before, after = (value.shape[:dim], value.shape[dim + 1 :])
+    return jnp.moveaxis(value.reshape(*before, size, -1, *after), dim, 0)
+
+
+def in_order(pieces, dim):
+    pieces = jnp.moveaxis(pieces, 0, dim)
+    shape = pieces.shape
+    return pieces.reshape(*shape[:dim], shape[dim] * shape[dim + 1], *shape[dim + 2 :])
+
+
+def swapped_with_each(x, axis, split_dim, concat_dim):
+    size, position = (lax.axis_size(axis), lax.axis_index(axis))
+    blocks = cut_along(x, split_dim, size)
+    outs = [blocks[position]]
+    for step in range(1, size):
+        sent = blocks[position ^ step]
+        outs.append(lax.ppermute(sent, axis, [(i, i ^ step) for i in range(size)]))
+    blocks = jnp.stack(outs)[position ^ jnp.arange(size)]
+    return in_order(blocks, concat_dim)
 
 
 def product(matrix_a, matrix_b):
@@ -49,7 +71,7 @@
 def layer_forward(states, weight_pair, graph, is_head):
     local_adj, halo_adj, inverse, send_index = graph
     outgoing = jnp.take(states, send_index, axis=0)
-    incoming = lax.all_to_all(outgoing, "dom", split_axis=0, concat_axis=0, tiled=True)
+    incoming = swapped_with_each(outgoing, "dom", 0, 0)
     halo_feats = incoming.reshape(-1, states.shape[1])
     summed = product(local_adj, states) + product(halo_adj, halo_feats)
     aggregated = (summed * inverse[:, None]).astype(jnp.bfloat16)

time: 490 us -> 533 us (1.088); the launches traced: 488 us -> 525 us
  starting transfers between devices: 33.2 us -> 91.7 us
  waiting for transfers between devices: 256 us -> 233 us
    ppermute x0 -> x45, starting transfers between devices: none -> 81 us  [swapped_with_each(): outs.append(lax.ppermute(sent, axis, [(i, i ^ step) for i in range(size)]))]
    unnamed x8, waiting for transfers between devices: 89.6 us -> 58.9 us
    all_to_all x3 -> x0, starting transfers between devices: 22 us -> none  [layer_forward(): lax.all_to_all(outgoing, 'dom', split_axis=0, concat_axis=0, tiled=True)]
    ppermute x0 -> x45, waiting for transfers between devices: none -> 21.2 us  [swapped_with_each(): outs.append(lax.ppermute(sent, axis, [(i, i ^ step) for i in range(size)]))]
    all_to_all x3 -> x0, waiting for transfers between devices: 12.9 us -> none  [layer_forward(): lax.all_to_all(outgoing, 'dom', split_axis=0, concat_axis=0, tiled=True)]
  transfers between devices with their start and end apart: 12 -> 54, of which waited for: 11 -> 18; matrix products, arithmetic and copies ran while one was open for 7% -> 7% of each run, Pallas kernels for 0% -> 0%
where the time goes in v1:
time: 533 us; the launch traced here: 525 us
  waiting for transfers between devices  233 us (44%)
  starting transfers between devices  91.7 us (17%)
  matrix products  57.5 us (11%)
  blocking collectives  56.6 us (11%)
  other arithmetic  43.7 us (8%)
  local copies, waits for them, and re-layouts  26 us (5%)
  between operations  16 us (3%)
    psum x1, waiting for transfers between devices, per_device(): summed_all = lax.psum(gradient, 'dom')  110 us
    ppermute x45, starting transfers between devices, swapped_with_each(): outs.append(lax.ppermute(sent, axis, [(i, i ^ step) for i in range(size)]))  81 us
    unnamed x8, waiting for transfers between devices  58.9 us
    psum x1, blocking collectives, per_device(): lax.psum((jnp.sum((log_total - picked) * weight_mask), jnp.sum(weight_mas...  42.8 us
    dot_general x12, matrix products, product(): return jnp.dot(matrix_a, matrix_b, preferred_element_type=jnp.float32)  26.1 us
    dot_general x10, matrix products, contract_rows(): lax.dot_general(matrix_a, matrix_b, (((0,), (0,)), ((), ())), preferred_e...  24.7 us
    ppermute x45, waiting for transfers between devices, swapped_with_each(): outs.append(lax.ppermute(sent, axis, [(i, i ^ step) for i in range(size)]))  21.2 us
    psum x1, waiting for transfers between devices, layer_forward(): mixed = lax.psum(partial_value, 'feat')  14.8 us
  transfers between devices with their start and end apart: 54, of which 18 were waited for; matrix products, arithmetic and copies ran while one was open for 7% of the time, Pallas kernels for 0%

profile of v1, /device:TPU:0, one launch (start us, length us, event | category | flops | bytes accessed | tf_op | source)
XLA Modules:
  0.0 525.0 jit_solution(11498293266345611539)
XLA Ops:
  11.1 3.0 collective-permute-start
  23.0 13.5 %fusion.43 = (s32[2048]{0:T(1024)S(1)}, bf16[2048,2048]{1,0:T(8,128)(2,1)S(1)}) fusion(s32[2048,2048]{1,0:T(8,128)} %param.12), kind=kLoop, calls=%fused_computation.234 | loop fusion | flops 8386560 | bytes 25174016 | tf_op jit(solution)/shard_map/reduce_sum | solution.py:148
  37.0 2.9 copy-done
  39.8 2.7 fusion.45
  42.5 2.6 collective-permute-start.5
  45.2 2.9 collective-permute-start.7
  49.4 3.5 collective-permute-start.9
  53.0 3.8 collective-permute-start.11
  58.0 4.6 collective-permute-start.13
  64.3 5.5 %collective-permute-done.14 = bf16[1,8,50]{2,1,0:T(8,128)(2,1)S(1)} collective-permute-done((bf16[1,8,50]{2,1,0:T(8,128)(2,1)S(1)}, bf16[1,8,50]{2,1,0:T(8,128)(2,1)S(1)}, u32[]{:S(2)}, u32[]{:S(2)}) %collective-permute-start.14) | collective-permute-done | bytes 832 | tf_op jit(solution)/shard_map/ppermute | solution.py:34
  70.8 58.7 %all-reduce.14.cloned.1.call-done = bf16[103680]{0:T(1024)(128)(2,1)} async-done(((bf16[103680]{0:T(1024)(128)(2,1)}), bf16[103680]{0:T(1024)(128)(2,1)}) %all-reduce.14.cloned.1.call-update) | async-done | bytes 207376
  137.4 6.7 %reduce-scatter.3.cloned.1.call-done = f32[2048,128]{0,1:T(8,128)} async-done(((f32[2048,256]{0,1:T(8,128)}), f32[2048,128]{0,1:T(8,128)}) %reduce-scatter.3.cloned.1.call-update) | async-done | bytes 1048592 | tf_op jit(solution)/shard_map/reduce_scatter | solution.py:83
  145.5 3.8 all-reduce.5
  151.4 7.3 %fusion.47 = f32[128,2048]{1,0:T(8,128)} fusion(bf16[2048,128]{0,1:T(8,128)(2,1)S(1)} %multiply_convert_fusion.3, bf16[2048,2048]{1,0:T(8,128)(2,1)} %copy-done), kind=kOutput, calls=%fused_computation.238 | convolution fusion | flops 1073741824 | bytes 9961472 | tf_op jit(solution)/shard_map/dot_general | solution.py:40
  167.8 2.5 collective-permute-start.20
  170.5 2.7 collective-permute-start.22
  174.7 3.3 collective-permute-start.24
  178.2 3.7 collective-permute-start.26
  183.3 4.2 collective-permute-start.28
  189.6 5.1 collective-permute-done.29
  197.7 2.7 convolution_add_fusion.1
  201.8 4.7 reduce-scatter.5.cloned.1.call-done
  207.8 3.3 all-reduce.4
  213.3 6.3 %fusion.49 = f32[128,2048]{1,0:T(8,128)S(1)} fusion(bf16[2048,128]{0,1:T(8,128)(2,1)S(1)} %multiply_convert_fusion.2, bf16[2048,2048]{1,0:T(8,128)(2,1)} %copy-done), kind=kOutput, calls=%fused_computation.240 | convolution fusion | flops 1073741824 | bytes 9961472 | tf_op jit(solution)/shard_map/dot_general | solution.py:40
  227.6 2.5 collective-permute-start.35
  230.2 2.7 collective-permute-start.37
  234.4 3.3 collective-permute-start.39
  237.9 3.7 collective-permute-start.41
  243.0 4.2 collective-permute-start.43
  249.3 5.1 collective-permute-done.44
  257.4 14.8 %all-reduce.10.cloned.1.call-done = f32[2048,47]{0,1:T(8,128)} async-done(((f32[2048,47]{0,1:T(8,128)}), f32[2048,47]{0,1:T(8,128)}) %all-reduce.10.cloned.1.call-update) | async-done | bytes 385040 | tf_op jit(solution)/shard_map/psum | solution.py:80
  275.0 42.8 %all-reduce.1 = (f32[]{:T(128)}, f32[]{:T(128)}) all-reduce(f32[]{:T(128)} %get-tuple-element.27, f32[]{:T(128)} %get-tuple-element.26), channel_id=1, replica_groups=mesh['dom'=16,'feat'=2] {'dom'}, use_global_device_ids=true, to_apply=%region_17.19 | all-reduce | flops 2 | bytes 16 | tf_op jit(solution)/shard_map/psum | solution.py:165
  320.0 7.9 %convolution_bitcast_fusion.2 = f32[2048,128]{1,0:T(8,128)} fusion(bf16[2048,128]{1,0:T(8,128)(2,1)S(1)} %fusion.5, bf16[2048,2048]{1,0:T(8,128)(2,1)} %copy-done), kind=kOutput, calls=%fused_computation.12 | convolution fusion | flops 1073741824 | bytes 9961472 | tf_op jit(solution)/shard_map/dot_general | solution.py:44
  328.9 3.5 all-to-all-start
  334.0 5.8 %all-to-all-done = bf16[16,8,128]{2,1,0:T(8,128)(2,1)S(1)} async-done(((bf16[16,8,128]{2,1,0:T(8,128)(2,1)}), bf16[16,8,128]{2,1,0:T(8,128)(2,1)S(1)}, u32[]{:S(2)}, u32[]{:S(2)}) %all-to-all-start) | async-done | bytes 32800 | tf_op jit(solution)/shard_map/all_to_all | solution.py:122
  342.8 3.0 multiply_reduce_fusion
  345.7 3.4 all-reduce.3
  350.3 5.7 %all-gather.3.cloned.1.call-done = bf16[2048,256]{0,1:T(8,128)(2,1)} async-done(((bf16[2048,128]{0,1:T(8,128)(2,1)}), bf16[2048,256]{0,1:T(8,128)(2,1)}) %all-gather.3.cloned.1.call-update) | async-done | bytes 1048592 | tf_op jit(solution)/shard_map/all_gather | solution.py:183
  358.0 7.8 %convolution_bitcast_fusion.1 = f32[2048,128]{1,0:T(8,128)} fusion(bf16[2048,128]{1,0:T(8,128)(2,1)S(1)} %fusion.2, bf16[2048,2048]{1,0:T(8,128)(2,1)} %copy-done), kind=kOutput, calls=%fused_computation.11 | convolution fusion | flops 1073741824 | bytes 9961472 | tf_op jit(solution)/shard_map/dot_general | solution.py:44
  366.7 6.9 %all-to-all-start.1 = ((bf16[16,8,128]{2,1,0:T(8,128)(2,1)}), bf16[16,8,128]{2,1,0:T(8,128)(2,1)S(1)}, u32[]{:S(2)}, u32[]{:S(2)}) async-start(bf16[16,8,128]{2,1,0:T(8,128)(2,1)} %fusion.10), calls=%async_computation.3 | async-start | bytes 65536 | tf_op jit(solution)/shard_map/all_to_all | solution.py:122
  373.7 2.7 convolution_add_fusion.5
  376.4 4.7 all-to-all-done.1
  381.1 3.5 scatter_custom_fusion.1
  384.5 2.6 copy.48
  387.2 3.3 multiply_reduce_fusion.1
  390.5 3.3 all-reduce.2
  393.7 2.3 multiply_convert_fusion
  406.7 109.6 %all-reduce.12.cloned.1.call-done = f32[1,103680]{1,0:T(1,128)} async-done(((f32[1,103680]{1,0:T(1,128)}), f32[1,103680]{1,0:T(1,128)}) %all-reduce.12.cloned.1.call-update) | async-done | bytes 414736 | tf_op jit(solution)/shard_map/psum | solution.py:198
  (292 shorter events, 94.1 us)
Async XLA Ops:
  7.2 122.4 %all-reduce.14.cloned.1.call-start = ((), (), s32[]{:S(2)}) async-start(), calls=%async_computation.10 | async-start | bytes 417792
  11.1 31.4 %collective-permute-start = (bf16[1,8,50]{2,1,0:T(8,128)(2,1)S(1)}, bf16[1,8,50]{2,1,0:T(8,128)(2,1)S(1)}, u32[]{:S(2)}, u32[]{:S(2)}) collective-permute-start(bf16[1,8,50]{2,1,0:T(8,128)(2,1)S(1)} %get-tuple-element.92), channel_id=1, source_target_pairs={{0,2},{2,0},{4,6},{6,4},{8,10},{10,8},{12,14},{14,12},{16,18},{18,... | collective-permute-start | bytes 2408 | tf_op jit(solution)/shard_map/ppermute | solution.py:34
  14.1 31.0 %collective-permute-start.1 = (bf16[1,8,50]{2,1,0:T(8,128)(2,1)S(1)}, bf16[1,8,50]{2,1,0:T(8,128)(2,1)S(1)}, u32[]{:S(2)}, u32[]{:S(2)}) collective-permute-start(bf16[1,8,50]{2,1,0:T(8,128)(2,1)S(1)} %get-tuple-element.91), channel_id=1, source_target_pairs={{0,4},{2,6},{4,0},{6,2},{8,12},{10,14},{12,8},{14,10},{16,20},{18,... | collective-permute-start | bytes 2408 | tf_op jit(solution)/shard_map/ppermute | solution.py:34
  15.7 29.6 %collective-permute-start.2 = (bf16[1,8,50]{2,1,0:T(8,128)(2,1)S(1)}, bf16[1,8,50]{2,1,0:T(8,128)(2,1)S(1)}, u32[]{:S(2)}, u32[]{:S(2)}) collective-permute-start(bf16[1,8,50]{2,1,0:T(8,128)(2,1)S(1)} %get-tuple-element.90), channel_id=1, source_target_pairs={{0,6},{2,4},{4,2},{6,0},{8,14},{10,12},{12,10},{14,8},{16,22},{18,... | collective-permute-start | bytes 2408 | tf_op jit(solution)/shard_map/ppermute | solution.py:34
  15.7 32.4 %collective-permute-start.3 = (bf16[1,8,50]{2,1,0:T(8,128)(2,1)S(1)}, bf16[1,8,50]{2,1,0:T(8,128)(2,1)S(1)}, u32[]{:S(2)}, u32[]{:S(2)}) collective-permute-start(bf16[1,8,50]{2,1,0:T(8,128)(2,1)S(1)} %get-tuple-element.89), channel_id=1, source_target_pairs={{0,8},{2,10},{4,12},{6,14},{8,0},{10,2},{12,4},{14,6},{16,24},{18,... | collective-permute-start | bytes 2408 | tf_op jit(solution)/shard_map/ppermute | solution.py:34
  17.7 31.7 %collective-permute-start.4 = (bf16[1,8,50]{2,1,0:T(8,128)(2,1)S(1)}, bf16[1,8,50]{2,1,0:T(8,128)(2,1)S(1)}, u32[]{:S(2)}, u32[]{:S(2)}) collective-permute-start(bf16[1,8,50]{2,1,0:T(8,128)(2,1)S(1)} %get-tuple-element.88), channel_id=1, source_target_pairs={{0,10},{2,8},{4,14},{6,12},{8,2},{10,0},{12,6},{14,4},{16,26},{18,... | collective-permute-start | bytes 2408 | tf_op jit(solution)/shard_map/ppermute | solution.py:34
  22.9 121.2 %reduce-scatter.3.cloned.1.call-start = ((), (), s32[]{:S(2)}) async-start(), calls=%async_computation.4 | async-start | bytes 3145728 | tf_op jit(solution)/shard_map/reduce_scatter | solution.py:83
  42.5 10.4 %collective-permute-start.5 = (bf16[1,8,50]{2,1,0:T(8,128)(2,1)S(1)}, bf16[1,8,50]{2,1,0:T(8,128)(2,1)S(1)}, u32[]{:S(2)}, u32[]{:S(2)}) collective-permute-start(bf16[1,8,50]{2,1,0:T(8,128)(2,1)S(1)} %get-tuple-element.87), channel_id=1, source_target_pairs={{0,12},{2,14},{4,8},{6,10},{8,4},{10,6},{12,0},{14,2},{16,28},{18,... | collective-permute-start | bytes 2408 | tf_op jit(solution)/shard_map/ppermute | solution.py:34
  45.1 7.9 %collective-permute-start.6 = (bf16[1,8,50]{2,1,0:T(8,128)(2,1)S(1)}, bf16[1,8,50]{2,1,0:T(8,128)(2,1)S(1)}, u32[]{:S(2)}, u32[]{:S(2)}) collective-permute-start(bf16[1,8,50]{2,1,0:T(8,128)(2,1)S(1)} %get-tuple-element.86), channel_id=1, source_target_pairs={{0,14},{2,12},{4,10},{6,8},{8,6},{10,4},{12,2},{14,0},{16,30},{18,... | collective-permute-start | bytes 2408 | tf_op jit(solution)/shard_map/ppermute | solution.py:34
  45.2 11.6 %collective-permute-start.7 = (bf16[1,8,50]{2,1,0:T(8,128)(2,1)S(1)}, bf16[1,8,50]{2,1,0:T(8,128)(2,1)S(1)}, u32[]{:S(2)}, u32[]{:S(2)}) collective-permute-start(bf16[1,8,50]{2,1,0:T(8,128)(2,1)S(1)} %get-tuple-element.85), channel_id=1, source_target_pairs={{0,16},{2,18},{4,20},{6,22},{8,24},{10,26},{12,28},{14,30},{16,0},... | collective-permute-start | bytes 2408 | tf_op jit(solution)/shard_map/ppermute | solution.py:34
  48.1 9.9 %collective-permute-start.8 = (bf16[1,8,50]{2,1,0:T(8,128)(2,1)S(1)}, bf16[1,8,50]{2,1,0:T(8,128)(2,1)S(1)}, u32[]{:S(2)}, u32[]{:S(2)}) collective-permute-start(bf16[1,8,50]{2,1,0:T(8,128)(2,1)S(1)} %get-tuple-element.84), channel_id=1, source_target_pairs={{0,18},{2,16},{4,22},{6,20},{8,26},{10,24},{12,30},{14,28},{16,2},... | collective-permute-start | bytes 2408 | tf_op jit(solution)/shard_map/ppermute | solution.py:34
  49.4 13.2 %collective-permute-start.9 = (bf16[1,8,50]{2,1,0:T(8,128)(2,1)S(1)}, bf16[1,8,50]{2,1,0:T(8,128)(2,1)S(1)}, u32[]{:S(2)}, u32[]{:S(2)}) collective-permute-start(bf16[1,8,50]{2,1,0:T(8,128)(2,1)S(1)} %get-tuple-element.83), channel_id=1, source_target_pairs={{0,20},{2,22},{4,16},{6,18},{8,28},{10,30},{12,24},{14,26},{16,4},... | collective-permute-start | bytes 2408 | tf_op jit(solution)/shard_map/ppermute | solution.py:34
  53.0 9.6 %collective-permute-start.10 = (bf16[1,8,50]{2,1,0:T(8,128)(2,1)S(1)}, bf16[1,8,50]{2,1,0:T(8,128)(2,1)S(1)}, u32[]{:S(2)}, u32[]{:S(2)}) collective-permute-start(bf16[1,8,50]{2,1,0:T(8,128)(2,1)S(1)} %get-tuple-element.82), channel_id=1, source_target_pairs={{0,22},{2,20},{4,18},{6,16},{8,30},{10,28},{12,26},{14,24},{16,6},... | collective-permute-start | bytes 2408 | tf_op jit(solution)/shard_map/ppermute | solution.py:34
  53.0 9.6 %collective-permute-start.11 = (bf16[1,8,50]{2,1,0:T(8,128)(2,1)S(1)}, bf16[1,8,50]{2,1,0:T(8,128)(2,1)S(1)}, u32[]{:S(2)}, u32[]{:S(2)}) collective-permute-start(bf16[1,8,50]{2,1,0:T(8,128)(2,1)S(1)} %get-tuple-element.81), channel_id=1, source_target_pairs={{0,24},{2,26},{4,28},{6,30},{8,16},{10,18},{12,20},{14,22},{16,8},... | collective-permute-start | bytes 2408 | tf_op jit(solution)/shard_map/ppermute | solution.py:34
  62.6 7.2 %collective-permute-start.14 = (bf16[1,8,50]{2,1,0:T(8,128)(2,1)S(1)}, bf16[1,8,50]{2,1,0:T(8,128)(2,1)S(1)}, u32[]{:S(2)}, u32[]{:S(2)}) collective-permute-start(bf16[1,8,50]{2,1,0:T(8,128)(2,1)S(1)} %get-tuple-element.78), channel_id=1, source_target_pairs={{0,30},{2,28},{4,26},{6,24},{8,22},{10,20},{12,18},{14,16},{16,14}... | collective-permute-start | bytes 2408 | tf_op jit(solution)/shard_map/ppermute | solution.py:34
  134.6 71.8 %reduce-scatter.5.cloned.1.call-start = ((), (), s32[]{:S(2)}) async-start(), calls=%async_computation.5 | async-start | bytes 3145728 | tf_op jit(solution)/shard_map/reduce_scatter | solution.py:83
  159.6 8.2 %collective-permute-start.15 = (bf16[1,8,128]{2,1,0:T(8,128)(2,1)S(1)}, bf16[1,8,128]{2,1,0:T(8,128)(2,1)S(1)}, u32[]{:S(2)}, u32[]{:S(2)}) collective-permute-start(bf16[1,8,128]{2,1,0:T(8,128)(2,1)S(1)} %get-tuple-element.77), channel_id=1, source_target_pairs={{0,2},{2,0},{4,6},{6,4},{8,10},{10,8},{12,14},{14,12},{16,18},{18,... | collective-permute-start | bytes 6152 | tf_op jit(solution)/shard_map/ppermute | solution.py:34
  161.5 8.8 %collective-permute-start.16 = (bf16[1,8,128]{2,1,0:T(8,128)(2,1)S(1)}, bf16[1,8,128]{2,1,0:T(8,128)(2,1)S(1)}, u32[]{:S(2)}, u32[]{:S(2)}) collective-permute-start(bf16[1,8,128]{2,1,0:T(8,128)(2,1)S(1)} %get-tuple-element.76), channel_id=1, source_target_pairs={{0,4},{2,6},{4,0},{6,2},{8,12},{10,14},{12,8},{14,10},{16,20},{18,... | collective-permute-start | bytes 6152 | tf_op jit(solution)/shard_map/ppermute | solution.py:34
  163.0 7.5 %collective-permute-start.17 = (bf16[1,8,128]{2,1,0:T(8,128)(2,1)S(1)}, bf16[1,8,128]{2,1,0:T(8,128)(2,1)S(1)}, u32[]{:S(2)}, u32[]{:S(2)}) collective-permute-start(bf16[1,8,128]{2,1,0:T(8,128)(2,1)S(1)} %get-tuple-element.75), channel_id=1, source_target_pairs={{0,6},{2,4},{4,2},{6,0},{8,14},{10,12},{12,10},{14,8},{16,22},{18,... | collective-permute-start | bytes 6152 | tf_op jit(solution)/shard_map/ppermute | solution.py:34
  163.2 10.0 %collective-permute-start.18 = (bf16[1,8,128]{2,1,0:T(8,128)(2,1)S(1)}, bf16[1,8,128]{2,1,0:T(8,128)(2,1)S(1)}, u32[]{:S(2)}, u32[]{:S(2)}) collective-permute-start(bf16[1,8,128]{2,1,0:T(8,128)(2,1)S(1)} %get-tuple-element.74), channel_id=1, source_target_pairs={{0,8},{2,10},{4,12},{6,14},{8,0},{10,2},{12,4},{14,6},{16,24},{18,... | collective-permute-start | bytes 6152 | tf_op jit(solution)/shard_map/ppermute | solution.py:34
  165.0 9.7 %collective-permute-start.19 = (bf16[1,8,128]{2,1,0:T(8,128)(2,1)S(1)}, bf16[1,8,128]{2,1,0:T(8,128)(2,1)S(1)}, u32[]{:S(2)}, u32[]{:S(2)}) collective-permute-start(bf16[1,8,128]{2,1,0:T(8,128)(2,1)S(1)} %get-tuple-element.73), channel_id=1, source_target_pairs={{0,10},{2,8},{4,14},{6,12},{8,2},{10,0},{12,6},{14,4},{16,26},{18,... | collective-permute-start | bytes 6152 | tf_op jit(solution)/shard_map/ppermute | solution.py:34
  167.8 10.2 %collective-permute-start.20 = (bf16[1,8,128]{2,1,0:T(8,128)(2,1)S(1)}, bf16[1,8,128]{2,1,0:T(8,128)(2,1)S(1)}, u32[]{:S(2)}, u32[]{:S(2)}) collective-permute-start(bf16[1,8,128]{2,1,0:T(8,128)(2,1)S(1)} %get-tuple-element.72), channel_id=1, source_target_pairs={{0,12},{2,14},{4,8},{6,10},{8,4},{10,6},{12,0},{14,2},{16,28},{18,... | collective-permute-start | bytes 6152 | tf_op jit(solution)/shard_map/ppermute | solution.py:34
  170.3 7.9 %collective-permute-start.21 = (bf16[1,8,128]{2,1,0:T(8,128)(2,1)S(1)}, bf16[1,8,128]{2,1,0:T(8,128)(2,1)S(1)}, u32[]{:S(2)}, u32[]{:S(2)}) collective-permute-start(bf16[1,8,128]{2,1,0:T(8,128)(2,1)S(1)} %get-tuple-element.71), channel_id=1, source_target_pairs={{0,14},{2,12},{4,10},{6,8},{8,6},{10,4},{12,2},{14,0},{16,30},{18,... | collective-permute-start | bytes 6152 | tf_op jit(solution)/shard_map/ppermute | solution.py:34
  170.5 11.4 %collective-permute-start.22 = (bf16[1,8,128]{2,1,0:T(8,128)(2,1)S(1)}, bf16[1,8,128]{2,1,0:T(8,128)(2,1)S(1)}, u32[]{:S(2)}, u32[]{:S(2)}) collective-permute-start(bf16[1,8,128]{2,1,0:T(8,128)(2,1)S(1)} %get-tuple-element.70), channel_id=1, source_target_pairs={{0,16},{2,18},{4,20},{6,22},{8,24},{10,26},{12,28},{14,30},{16,0},... | collective-permute-start | bytes 6152 | tf_op jit(solution)/shard_map/ppermute | solution.py:34
  173.2 10.1 %collective-permute-start.23 = (bf16[1,8,128]{2,1,0:T(8,128)(2,1)S(1)}, bf16[1,8,128]{2,1,0:T(8,128)(2,1)S(1)}, u32[]{:S(2)}, u32[]{:S(2)}) collective-permute-start(bf16[1,8,128]{2,1,0:T(8,128)(2,1)S(1)} %get-tuple-element.69), channel_id=1, source_target_pairs={{0,18},{2,16},{4,22},{6,20},{8,26},{10,24},{12,30},{14,28},{16,2},... | collective-permute-start | bytes 6152 | tf_op jit(solution)/shard_map/ppermute | solution.py:34
  174.7 12.8 %collective-permute-start.24 = (bf16[1,8,128]{2,1,0:T(8,128)(2,1)S(1)}, bf16[1,8,128]{2,1,0:T(8,128)(2,1)S(1)}, u32[]{:S(2)}, u32[]{:S(2)}) collective-permute-start(bf16[1,8,128]{2,1,0:T(8,128)(2,1)S(1)} %get-tuple-element.68), channel_id=1, source_target_pairs={{0,20},{2,22},{4,16},{6,18},{8,28},{10,30},{12,24},{14,26},{16,4},... | collective-permute-start | bytes 6152 | tf_op jit(solution)/shard_map/ppermute | solution.py:34
  178.0 9.7 %collective-permute-start.25 = (bf16[1,8,128]{2,1,0:T(8,128)(2,1)S(1)}, bf16[1,8,128]{2,1,0:T(8,128)(2,1)S(1)}, u32[]{:S(2)}, u32[]{:S(2)}) collective-permute-start(bf16[1,8,128]{2,1,0:T(8,128)(2,1)S(1)} %get-tuple-element.67), channel_id=1, source_target_pairs={{0,22},{2,20},{4,18},{6,16},{8,30},{10,28},{12,26},{14,24},{16,6},... | collective-permute-start | bytes 6152 | tf_op jit(solution)/shard_map/ppermute | solution.py:34
  178.2 9.5 %collective-permute-start.26 = (bf16[1,8,128]{2,1,0:T(8,128)(2,1)S(1)}, bf16[1,8,128]{2,1,0:T(8,128)(2,1)S(1)}, u32[]{:S(2)}, u32[]{:S(2)}) collective-permute-start(bf16[1,8,128]{2,1,0:T(8,128)(2,1)S(1)} %get-tuple-element.66), channel_id=1, source_target_pairs={{0,24},{2,26},{4,28},{6,30},{8,16},{10,18},{12,20},{14,22},{16,8},... | collective-permute-start | bytes 6152 | tf_op jit(solution)/shard_map/ppermute | solution.py:34
  187.5 7.2 %collective-permute-start.29 = (bf16[1,8,128]{2,1,0:T(8,128)(2,1)S(1)}, bf16[1,8,128]{2,1,0:T(8,128)(2,1)S(1)}, u32[]{:S(2)}, u32[]{:S(2)}) collective-permute-start(bf16[1,8,128]{2,1,0:T(8,128)(2,1)S(1)} %get-tuple-element.63), channel_id=1, source_target_pairs={{0,30},{2,28},{4,26},{6,24},{8,22},{10,20},{12,18},{14,16},{16,14}... | collective-permute-start | bytes 6152 | tf_op jit(solution)/shard_map/ppermute | solution.py:34
  200.4 71.8 %all-reduce.10.cloned.1.call-start = ((), (), s32[]{:S(2)}) async-start(), calls=%async_computation.6 | async-start | bytes 786432 | tf_op jit(solution)/shard_map/psum | solution.py:80
  220.4 7.1 %collective-permute-start.30 = (bf16[1,8,128]{2,1,0:T(8,128)(2,1)S(1)}, bf16[1,8,128]{2,1,0:T(8,128)(2,1)S(1)}, u32[]{:S(2)}, u32[]{:S(2)}) collective-permute-start(bf16[1,8,128]{2,1,0:T(8,128)(2,1)S(1)} %get-tuple-element.62), channel_id=1, source_target_pairs={{0,2},{2,0},{4,6},{6,4},{8,10},{10,8},{12,14},{14,12},{16,18},{18,... | collective-permute-start | bytes 6152 | tf_op jit(solution)/shard_map/ppermute | solution.py:34
  222.3 7.7 %collective-permute-start.31 = (bf16[1,8,128]{2,1,0:T(8,128)(2,1)S(1)}, bf16[1,8,128]{2,1,0:T(8,128)(2,1)S(1)}, u32[]{:S(2)}, u32[]{:S(2)}) collective-permute-start(bf16[1,8,128]{2,1,0:T(8,128)(2,1)S(1)} %get-tuple-element.61), channel_id=1, source_target_pairs={{0,4},{2,6},{4,0},{6,2},{8,12},{10,14},{12,8},{14,10},{16,20},{18,... | collective-permute-start | bytes 6152 | tf_op jit(solution)/shard_map/ppermute | solution.py:34
  223.8 6.4 %collective-permute-start.32 = (bf16[1,8,128]{2,1,0:T(8,128)(2,1)S(1)}, bf16[1,8,128]{2,1,0:T(8,128)(2,1)S(1)}, u32[]{:S(2)}, u32[]{:S(2)}) collective-permute-start(bf16[1,8,128]{2,1,0:T(8,128)(2,1)S(1)} %get-tuple-element.60), channel_id=1, source_target_pairs={{0,6},{2,4},{4,2},{6,0},{8,14},{10,12},{12,10},{14,8},{16,22},{18,... | collective-permute-start | bytes 6152 | tf_op jit(solution)/shard_map/ppermute | solution.py:34
  224.0 9.0 %collective-permute-start.33 = (bf16[1,8,128]{2,1,0:T(8,128)(2,1)S(1)}, bf16[1,8,128]{2,1,0:T(8,128)(2,1)S(1)}, u32[]{:S(2)}, u32[]{:S(2)}) collective-permute-start(bf16[1,8,128]{2,1,0:T(8,128)(2,1)S(1)} %get-tuple-element.59), channel_id=1, source_target_pairs={{0,8},{2,10},{4,12},{6,14},{8,0},{10,2},{12,4},{14,6},{16,24},{18,... | collective-permute-start | bytes 6152 | tf_op jit(solution)/shard_map/ppermute | solution.py:34
  225.8 8.6 %collective-permute-start.34 = (bf16[1,8,128]{2,1,0:T(8,128)(2,1)S(1)}, bf16[1,8,128]{2,1,0:T(8,128)(2,1)S(1)}, u32[]{:S(2)}, u32[]{:S(2)}) collective-permute-start(bf16[1,8,128]{2,1,0:T(8,128)(2,1)S(1)} %get-tuple-element.58), channel_id=1, source_target_pairs={{0,10},{2,8},{4,14},{6,12},{8,2},{10,0},{12,6},{14,4},{16,26},{18,... | collective-permute-start | bytes 6152 | tf_op jit(solution)/shard_map/ppermute | solution.py:34
  227.6 10.2 %collective-permute-start.35 = (bf16[1,8,128]{2,1,0:T(8,128)(2,1)S(1)}, bf16[1,8,128]{2,1,0:T(8,128)(2,1)S(1)}, u32[]{:S(2)}, u32[]{:S(2)}) collective-permute-start(bf16[1,8,128]{2,1,0:T(8,128)(2,1)S(1)} %get-tuple-element.57), channel_id=1, source_target_pairs={{0,12},{2,14},{4,8},{6,10},{8,4},{10,6},{12,0},{14,2},{16,28},{18,... | collective-permute-start | bytes 6152 | tf_op jit(solution)/shard_map/ppermute | solution.py:34
  230.0 7.9 %collective-permute-start.36 = (bf16[1,8,128]{2,1,0:T(8,128)(2,1)S(1)}, bf16[1,8,128]{2,1,0:T(8,128)(2,1)S(1)}, u32[]{:S(2)}, u32[]{:S(2)}) collective-permute-start(bf16[1,8,128]{2,1,0:T(8,128)(2,1)S(1)} %get-tuple-element.56), channel_id=1, source_target_pairs={{0,14},{2,12},{4,10},{6,8},{8,6},{10,4},{12,2},{14,0},{16,30},{18,... | collective-permute-start | bytes 6152 | tf_op jit(solution)/shard_map/ppermute | solution.py:34
  230.2 11.4 %collective-permute-start.37 = (bf16[1,8,128]{2,1,0:T(8,128)(2,1)S(1)}, bf16[1,8,128]{2,1,0:T(8,128)(2,1)S(1)}, u32[]{:S(2)}, u32[]{:S(2)}) collective-permute-start(bf16[1,8,128]{2,1,0:T(8,128)(2,1)S(1)} %get-tuple-element.55), channel_id=1, source_target_pairs={{0,16},{2,18},{4,20},{6,22},{8,24},{10,26},{12,28},{14,30},{16,0},... | collective-permute-start | bytes 6152 | tf_op jit(solution)/shard_map/ppermute | solution.py:34
  233.0 10.0 %collective-permute-start.38 = (bf16[1,8,128]{2,1,0:T(8,128)(2,1)S(1)}, bf16[1,8,128]{2,1,0:T(8,128)(2,1)S(1)}, u32[]{:S(2)}, u32[]{:S(2)}) collective-permute-start(bf16[1,8,128]{2,1,0:T(8,128)(2,1)S(1)} %get-tuple-element.54), channel_id=1, source_target_pairs={{0,18},{2,16},{4,22},{6,20},{8,26},{10,24},{12,30},{14,28},{16,2},... | collective-permute-start | bytes 6152 | tf_op jit(solution)/shard_map/ppermute | solution.py:34
  234.4 12.8 %collective-permute-start.39 = (bf16[1,8,128]{2,1,0:T(8,128)(2,1)S(1)}, bf16[1,8,128]{2,1,0:T(8,128)(2,1)S(1)}, u32[]{:S(2)}, u32[]{:S(2)}) collective-permute-start(bf16[1,8,128]{2,1,0:T(8,128)(2,1)S(1)} %get-tuple-element.53), channel_id=1, source_target_pairs={{0,20},{2,22},{4,16},{6,18},{8,28},{10,30},{12,24},{14,26},{16,4},... | collective-permute-start | bytes 6152 | tf_op jit(solution)/shard_map/ppermute | solution.py:34
  237.8 9.7 %collective-permute-start.40 = (bf16[1,8,128]{2,1,0:T(8,128)(2,1)S(1)}, bf16[1,8,128]{2,1,0:T(8,128)(2,1)S(1)}, u32[]{:S(2)}, u32[]{:S(2)}) collective-permute-start(bf16[1,8,128]{2,1,0:T(8,128)(2,1)S(1)} %get-tuple-element.52), channel_id=1, source_target_pairs={{0,22},{2,20},{4,18},{6,16},{8,30},{10,28},{12,26},{14,24},{16,6},... | collective-permute-start | bytes 6152 | tf_op jit(solution)/shard_map/ppermute | solution.py:34
  237.9 9.5 %collective-permute-start.41 = (bf16[1,8,128]{2,1,0:T(8,128)(2,1)S(1)}, bf16[1,8,128]{2,1,0:T(8,128)(2,1)S(1)}, u32[]{:S(2)}, u32[]{:S(2)}) collective-permute-start(bf16[1,8,128]{2,1,0:T(8,128)(2,1)S(1)} %get-tuple-element.51), channel_id=1, source_target_pairs={{0,24},{2,26},{4,28},{6,30},{8,16},{10,18},{12,20},{14,22},{16,8},... | collective-permute-start | bytes 6152 | tf_op jit(solution)/shard_map/ppermute | solution.py:34
  247.3 7.2 %collective-permute-start.44 = (bf16[1,8,128]{2,1,0:T(8,128)(2,1)S(1)}, bf16[1,8,128]{2,1,0:T(8,128)(2,1)S(1)}, u32[]{:S(2)}, u32[]{:S(2)}) collective-permute-start(bf16[1,8,128]{2,1,0:T(8,128)(2,1)S(1)} %get-tuple-element.48), channel_id=1, source_target_pairs={{0,30},{2,28},{4,26},{6,24},{8,22},{10,20},{12,18},{14,16},{16,14}... | collective-permute-start | bytes 6152 | tf_op jit(solution)/shard_map/ppermute | solution.py:34
  328.9 10.9 %all-to-all-start = ((bf16[16,8,128]{2,1,0:T(8,128)(2,1)}), bf16[16,8,128]{2,1,0:T(8,128)(2,1)S(1)}, u32[]{:S(2)}, u32[]{:S(2)}) async-start(bf16[16,8,128]{2,1,0:T(8,128)(2,1)} %fusion.9), calls=%async_computation.2 | async-start | bytes 65536 | tf_op jit(solution)/shard_map/all_to_all | solution.py:122
  332.4 23.6 %all-gather.3.cloned.1.call-start = ((), (), s32[]{:S(2)}) async-start(), calls=%async_computation.7 | async-start | bytes 1572864 | tf_op jit(solution)/shard_map/all_gather | solution.py:183
  366.7 14.3 %all-to-all-start.1 = ((bf16[16,8,128]{2,1,0:T(8,128)(2,1)}), bf16[16,8,128]{2,1,0:T(8,128)(2,1)S(1)}, u32[]{:S(2)}, u32[]{:S(2)}) async-start(bf16[16,8,128]{2,1,0:T(8,128)(2,1)} %fusion.10), calls=%async_computation.3 | async-start | bytes 65536 | tf_op jit(solution)/shard_map/all_to_all | solution.py:122
  373.7 28.3 %all-gather.5.cloned.1.call-start = ((), (), s32[]{:S(2)}) async-start(), calls=%async_computation.8 | async-start | bytes 1572864 | tf_op jit(solution)/shard_map/all_gather | solution.py:183
  396.1 120.2 %all-reduce.12.cloned.1.call-start = ((), (), s32[]{:S(2)}) async-start(), calls=%async_computation.9 | async-start | bytes 829440 | tf_op jit(solution)/shard_map/psum | solution.py:198
  (34 other events, 1235.3 us)
Sparse Core Ops, SparseCore 0:
  23.1 106.4 all-reduce.13
  134.8 9.3 reduce-scatter.2
  200.5 5.9 reduce-scatter.4
  257.4 14.7 all-reduce.9
  350.4 5.5 all-gather.2
  396.2 5.6 all-gather.4
  407.1 109.1 all-reduce.11
